TPU v7x, 32 devices: a whole 2x2x4 slice. The times are simulated.
32 devices in a mesh: blk: 8 (over y, x, core), dp: 4 (over z).
Axes of the slice: x: 2, y: 2, z: 4, core: 2. Of those that a mesh axis runs over, the one named last changes fastest.
Arguments:
- normed_input: bfloat16 [32, 256, 5120], P(('blk', 'dp')), may hold values from -40 to 40
- segment_ids: int32 [4, 8, 256], P('dp'), may hold values from 0 to 3, never falling along the last dimension, each value on 1 to 128 neighbouring positions
- weights_qkv: bfloat16 [8, 5120, 384], P('blk'), may hold values from -0.08385255 to 0.08385255
- weights_out: bfloat16 [8, 128, 5120], P('blk'), may hold values from -0.5 to 0.5
- cotangent: bfloat16 [32, 256, 5120], P(('blk', 'dp')), may hold values from -6 to 6
Outputs:
- input_grad: bfloat16 [32, 256, 5120], P(('blk', 'dp'))
- grad_qkv: bfloat16 [8, 5120, 384], P('blk', 'dp')
- grad_out: bfloat16 [8, 128, 5120], P('blk', None, 'dp')
All inputs are finite; a program needn't handle non-finite values.
Results may differ from a plain program's by a relative error of at most 0.02.
Values may be sent and summed in bfloat16 or wider, within the bound.
A program may use at most 128 MiB of HBM per device.

v0:
```python
import jax
import jax.numpy as jnp
from jax import lax
from jax.sharding import PartitionSpec as P


def shifted(block, axis, distance):
    devices = range(lax.axis_size(axis))
    route = [((i - distance) % len(devices), i) for i in devices]
    return lax.ppermute(block, axis, route)


def group_terms(inputs, seg_row, w_qkv, w_out, grad_in):
    head = w_out.shape[0]
    scale = head ** (-0.5)
    qkv = jnp.dot(inputs, w_qkv, preferred_element_type=jnp.float32).astype(jnp.bfloat16)
    query = qkv[:, :head]
    keys = qkv[:, head : 2 * head]
    values = qkv[:, 2 * head :]
    count = inputs.shape[0]
    places = jnp.arange(count, dtype=jnp.int32)
    allowed = (places[:, None] >= places[None, :]) & (seg_row[:, None] == seg_row[None, :])
    scores = jnp.dot(query, keys.T, preferred_element_type=jnp.float32) * scale
    scores = jnp.where(allowed, scores, jnp.float32(-1e30))
    top = jnp.max(scores, axis=-1, keepdims=True)
    expo = jnp.where(allowed, jnp.exp(scores - top), jnp.float32(0.0))
    probs = expo / jnp.sum(expo, axis=-1, keepdims=True)
    probs_b = probs.astype(jnp.bfloat16)
    attended = jnp.dot(probs_b, values, preferred_element_type=jnp.float32).astype(jnp.bfloat16)
    grad_wout = jnp.dot(attended.T, grad_in, preferred_element_type=jnp.float32)
    d_att = jnp.dot(grad_in, w_out.T, preferred_element_type=jnp.float32).astype(jnp.bfloat16)
    d_probs = jnp.dot(d_att, values.T, preferred_element_type=jnp.float32)
    d_scores = (
        probs * (d_probs - jnp.sum(probs * d_probs, axis=-1, keepdims=True)) * scale
    ).astype(jnp.bfloat16)
    d_query = jnp.dot(d_scores, keys, preferred_element_type=jnp.float32)
    d_keys = jnp.dot(d_scores.T, query, preferred_element_type=jnp.float32)
    d_values = jnp.dot(probs_b.T, d_att, preferred_element_type=jnp.float32)
    d_qkv = jnp.concatenate([d_query, d_keys, d_values], axis=1).astype(jnp.bfloat16)
    grad_wqkv = jnp.dot(inputs.T, d_qkv, preferred_element_type=jnp.float32)
    input_term = jnp.dot(d_qkv, w_qkv.T, preferred_element_type=jnp.float32)
    return (input_term, grad_wqkv, grad_wout)


def local(normed_input, segment_ids, weights_qkv, weights_out, cotangent):
    inputs = normed_input[0]
    grad_in = cotangent[0]
    here = lax.axis_index("blk")
    seg_table = segment_ids[0]
    own_seg = lax.dynamic_index_in_dim(seg_table, here, 0, keepdims=False)
    own_qkv = weights_qkv[0]
    own_out = weights_out[0]
    moved_qkv, moved_out = shifted((weights_qkv, weights_out), "blk", 1)
    term_own, gq_own, go_own = group_terms(inputs, own_seg, own_qkv, own_out, grad_in)
    term_far, gq_far, go_far = group_terms(inputs, own_seg, moved_qkv[0], moved_out[0], grad_in)
    input_grad = (term_own + term_far).astype(jnp.bfloat16)
    back_qkv, back_out = (
        shifted(gq_far.astype(jnp.bfloat16), "blk", -1).astype(gq_far.dtype),
        shifted(go_far.astype(jnp.bfloat16), "blk", -1).astype(go_far.dtype),
    )
    total_qkv, total_out = (
        lax.psum_scatter(
            (gq_own + back_qkv)[None].astype(jnp.bfloat16), "dp", scatter_dimension=1, tiled=True
        ).astype(jnp.float32),
        lax.psum_scatter(
            (go_own + back_out)[None].astype(jnp.bfloat16), "dp", scatter_dimension=2, tiled=True
        ).astype(jnp.float32),
    )
    return (input_grad[None], total_qkv.astype(jnp.bfloat16), total_out.astype(jnp.bfloat16))


def solution(mesh):
    placed = (
        P(("blk", "dp"), None, None),
        P("dp", None, None),
        P("blk", None, None),
        P("blk", None, None),
        P(("blk", "dp"), None, None),
    )
    return jax.shard_map(
        local,
        mesh=mesh,
        in_specs=placed,
        out_specs=(P(("blk", "dp"), None, None), P("blk", "dp", None), P("blk", None, "dp")),
        check_vma=False,
    )
```

profile of v0, /device:TPU:1, one launch (start us, length us, event | category | flops | bytes accessed | tf_op | source)
XLA Modules:
  0.0 239.5 jit_solution(15633072029519640928)
XLA Ops:
  7.2 2.7 %collective-permute-start = (bf16[1,5120,384]{2,1,0:T(8,128)(2,1)}, bf16[1,5120,384]{2,1,0:T(8,128)(2,1)}, u32[]{:S(2)}, u32[]{:S(2)}) collective-permute-start(bf16[1,5120,384]{2,1,0:T(8,128)(2,1)} %param.7), channel_id=1, source_target_pairs={{28,0},{0,4},{4,8},{8,12},{12,16},{16,20},{20,24},{24,28},{29,1},{... | collective-permute-start | bytes 11796488 | tf_op jit(solution)/shard_map/ppermute | solution.py:10
  9.9 0.1 collective-permute-start.1
  9.9 0.7 constant_dynamic-slice_fusion
  10.7 3.8 %fusion.26 = bf16[256,384]{1,0:T(8,128)(2,1)S(1)} fusion(bf16[1,5120,384]{2,1,0:T(8,128)(2,1)} %param.7, bf16[1,256,5120]{2,1,0:T(8,128)(2,1)S(1)} %copy-done), kind=kOutput, calls=%fused_computation.31 | convolution fusion | flops 1006731264 | bytes 6750208 | tf_op jit(solution)/shard_map/dot_general | solution.py:16
  14.5 0.2 fusion.88
  14.7 0.8 fusion.38
  15.6 51.3 %collective-permute-done.1 = bf16[1,128,5120]{2,1,0:T(8,128)(2,1)} collective-permute-done((bf16[1,128,5120]{2,1,0:T(8,128)(2,1)}, bf16[1,128,5120]{2,1,0:T(8,128)(2,1)}, u32[]{:S(2)}, u32[]{:S(2)}) %collective-permute-start.1) | collective-permute-done | bytes 1310752 | tf_op jit(solution)/shard_map/ppermute | solution.py:10
  66.9 2.2 fusion.43
  69.1 3.6 %fusion.31 = bf16[256,384]{1,0:T(8,128)(2,1)S(1)} fusion(bf16[1,5120,384]{2,1,0:T(8,128)(2,1)} %collective-permute-done, bf16[1,256,5120]{2,1,0:T(8,128)(2,1)S(1)} %copy-done), kind=kOutput, calls=%fused_computation.32 | convolution fusion | flops 1006731264 | bytes 6750208 | tf_op jit(solution)/shard_map/dot_general | solution.py:16
  72.7 0.2 fusion.87
  73.0 0.1 fusion.54
  73.1 0.3 convolution_convert_fusion.4
  73.4 0.2 multiply_reduce_fusion
  73.6 0.2 multiply_reduce_fusion.1
  73.9 0.2 multiply_convert_fusion
  74.1 0.2 convolution_convert_fusion.5
  74.3 0.2 convolution_convert_fusion.6
  74.5 1.2 fusion.2
  75.7 1.6 collective-permute-start.2
  77.3 0.2 convolution_convert_fusion.8
  77.5 0.2 convolution_convert_fusion.9
  77.8 0.3 convolution_convert_fusion.7
  78.1 43.6 %collective-permute-done.2 = bf16[5120,384]{0,1:T(8,128)(2,1)S(1)} collective-permute-done((bf16[5120,384]{0,1:T(8,128)(2,1)S(1)}, bf16[5120,384]{0,1:T(8,128)(2,1)S(1)}, u32[]{:S(2)}, u32[]{:S(2)}) %collective-permute-start.2) | collective-permute-done | bytes 3932192 | tf_op jit(solution)/shard_map/ppermute | solution.py:10
  121.6 3.2 %fusion.3 = bf16[1,5120,384]{1,2,0:T(8,128)(2,1)} fusion(bf16[5120,384]{0,1:T(8,128)(2,1)S(1)} %collective-permute-done.2, bf16[1,256,5120]{2,1,0:T(8,128)(2,1)S(1)} %copy-done, bf16[256,128]{0,1:T(8,128)(2,1)S(1)} %convolution_convert_fusion.7, bf16[256,128]{0,1:T(8,128)(2,1)S(1)} %convolution_convert_fusion.8, ...), kind=kOutput, calls=%fused_computation.6 | convolution fusion | flops 1013121024 | bytes 10682368 | tf_op jit(solution)/shard_map/dot_general | solution.py:40
  124.9 3.7 %convolution_convert_fusion.1 = bf16[128,5120]{1,0:T(8,128)(2,1)} fusion(bf16[1,256,5120]{2,1,0:T(8,128)(2,1)} %param.9, bf16[256,384]{1,0:T(8,128)(2,1)} %copy-done.4, f32[256,256]{0,1:T(8,128)S(1)} %get-tuple-element.11, f32[256]{0:T(256)S(1)} %fusion.54, f32[256]{0:T(256)S(1)} %get-tuple-element.10, s32[256]{0:T(256)S(1)} %bitcast.83), kind=kOutput, calls=%fused_computation.8 | convolution fusion | flops 353468416 | bytes 4263936 | tf_op jit(solution)/shard_map/dot_general | solution.py:30
  128.6 17.6 %collective-permute-done.3 = bf16[128,5120]{1,0:T(8,128)(2,1)} collective-permute-done((bf16[128,5120]{1,0:T(8,128)(2,1)}, bf16[128,5120]{1,0:T(8,128)(2,1)}, u32[]{:S(2)}, u32[]{:S(2)}) %collective-permute-start.3) | collective-permute-done | bytes 1310752 | tf_op jit(solution)/shard_map/ppermute | solution.py:10
  146.3 4.2 %fusion.23 = bf16[1,128,5120]{2,1,0:T(8,128)(2,1)} fusion(bf16[128,5120]{1,0:T(8,128)(2,1)} %collective-permute-done.3, bf16[1,256,5120]{2,1,0:T(8,128)(2,1)} %param.9, bf16[256,384]{1,0:T(8,128)(2,1)} %copy-done.3, f32[256,256]{0,1:T(8,128)S(1)} %get-tuple-element.13, f32[256]{0:T(256)} %copy-done.5, f32[256]{0:T(256)S(1)} %get-tuple-element.12, ...), kind=kOutput, calls=%fused_computation.28 | convolution fusion | flops 354779136 | bytes 5574656 | tf_op jit(solution)/shard_map/dot_general | solution.py:30
  150.5 3.7 %fusion.8 = f32[256,5120]{1,0:T(8,128)S(1)} fusion(bf16[1,5120,384]{2,1,0:T(8,128)(2,1)} %param.7, bf16[256,128]{0,1:T(8,128)(2,1)S(1)} %convolution_convert_fusion.7, bf16[256,128]{0,1:T(8,128)(2,1)S(1)} %convolution_convert_fusion.8, bf16[256,128]{0,1:T(8,128)(2,1)S(1)} %convolution_convert_fusion.9), kind=kOutput, calls=%fused_computation.12 | convolution fusion | flops 1007222784 | bytes 9371648 | tf_op jit(solution)/shard_map/dot_general | solution.py:41
  154.2 5.2 %fusion.4 = bf16[1,256,5120]{2,1,0:T(8,128)(2,1)} fusion(f32[256,5120]{1,0:T(8,128)S(1)} %fusion.8, bf16[1,5120,384]{2,1,0:T(8,128)(2,1)} %collective-permute-done, bf16[256,128]{0,1:T(8,128)(2,1)S(1)} %convolution_convert_fusion.4, bf16[256,128]{0,1:T(8,128)(2,1)S(1)} %convolution_convert_fusion.5, bf16[256,128]{0,1:T(8,128)(2,1)S(1)} %convolution_convert_fusion.6), kind=kOutput, calls=%fused_computation.7 | convolution fusion | flops 1009844224 | bytes 11993088 | tf_op jit(solution)/shard_map/dot_general | solution.py:41
  159.4 38.6 %reduce-scatter.3.cloned.1.call-done = bf16[1,1280,384]{1,2,0:T(8,128)(2,1)} async-done(((bf16[1,5120,384]{1,2,0:T(8,128)(2,1)}), bf16[1,1280,384]{1,2,0:T(8,128)(2,1)}) %reduce-scatter.3.cloned.1.call-update) | async-done | bytes 983056 | tf_op jit(solution)/shard_map/reduce_scatter | solution.py:62
  198.0 2.2 copy.8
  200.2 32.4 %reduce-scatter.5.cloned.1.call-done = bf16[1,128,1280]{2,1,0:T(8,128)(2,1)} async-done(((bf16[1,128,5120]{2,1,0:T(8,128)(2,1)}), bf16[1,128,1280]{2,1,0:T(8,128)(2,1)}) %reduce-scatter.5.cloned.1.call-update) | async-done | bytes 327696 | tf_op jit(solution)/shard_map/reduce_scatter | solution.py:65
  (18 shorter events, 0.2 us)
Async XLA Ops:
  7.2 3.5 %copy-start = (bf16[1,256,5120]{2,1,0:T(8,128)(2,1)S(1)}, bf16[1,256,5120]{2,1,0:T(8,128)(2,1)}, u32[]{:S(2)}) copy-start(bf16[1,256,5120]{2,1,0:T(8,128)(2,1)} %param.5) | copy-start | bytes 7864324
  7.2 190.8 %reduce-scatter.3.cloned.1.call-start = ((), (), s32[]{:S(2)}) async-start(), calls=%async_computation.2 | async-start | bytes 4915200 | tf_op jit(solution)/shard_map/reduce_scatter | solution.py:62
  7.2 61.9 %collective-permute-start = (bf16[1,5120,384]{2,1,0:T(8,128)(2,1)}, bf16[1,5120,384]{2,1,0:T(8,128)(2,1)}, u32[]{:S(2)}, u32[]{:S(2)}) collective-permute-start(bf16[1,5120,384]{2,1,0:T(8,128)(2,1)} %param.7), channel_id=1, source_target_pairs={{28,0},{0,4},{4,8},{8,12},{12,16},{16,20},{20,24},{24,28},{29,1},{... | collective-permute-start | bytes 11796488 | tf_op jit(solution)/shard_map/ppermute | solution.py:10
  9.9 57.0 %collective-permute-start.1 = (bf16[1,128,5120]{2,1,0:T(8,128)(2,1)}, bf16[1,128,5120]{2,1,0:T(8,128)(2,1)}, u32[]{:S(2)}, u32[]{:S(2)}) collective-permute-start(bf16[1,128,5120]{2,1,0:T(8,128)(2,1)} %param.8), channel_id=1, source_target_pairs={{28,0},{0,4},{4,8},{8,12},{12,16},{16,20},{20,24},{24,28},{29,1},{... | collective-permute-start | bytes 3932168 | tf_op jit(solution)/shard_map/ppermute | solution.py:10
  10.7 4.0 %copy-start.1 = (bf16[1,256,5120]{2,1,0:T(8,128)(2,1)S(1)}, bf16[1,256,5120]{2,1,0:T(8,128)(2,1)}, u32[]{:S(2)}) copy-start(bf16[1,256,5120]{2,1,0:T(8,128)(2,1)} %param.9) | copy-start | bytes 7864324
  10.7 4.0 %copy-start.2 = (bf16[1,128,5120]{2,1,0:T(8,128)(2,1)S(1)}, bf16[1,128,5120]{2,1,0:T(8,128)(2,1)}, u32[]{:S(2)}) copy-start(bf16[1,128,5120]{2,1,0:T(8,128)(2,1)} %param.8) | copy-start | bytes 3932164
  14.5 63.1 %copy-start.3 = (bf16[256,384]{1,0:T(8,128)(2,1)}, bf16[256,384]{1,0:T(8,128)(2,1)S(1)}, u32[]{:S(2)}) copy-start(bf16[256,384]{1,0:T(8,128)(2,1)S(1)} %fusion.26) | copy-start | bytes 589828
  72.7 1.6 copy-start.4
  73.6 4.1 %copy-start.5 = (f32[256]{0:T(256)}, f32[256]{0:T(256)S(1)}, u32[]{:S(2)}) copy-start(f32[256]{0:T(256)S(1)} %get-tuple-element.7) | copy-start | bytes 3076
  75.7 45.9 %collective-permute-start.2 = (bf16[5120,384]{0,1:T(8,128)(2,1)S(1)}, bf16[5120,384]{0,1:T(8,128)(2,1)S(1)}, u32[]{:S(2)}, u32[]{:S(2)}) collective-permute-start(bf16[5120,384]{0,1:T(8,128)(2,1)S(1)} %fusion.2), channel_id=1, source_target_pairs={{4,0},{8,4},{12,8},{16,12},{20,16},{24,20},{28,24},{0,28},{5,1},{9... | collective-permute-start | bytes 11796488 | tf_op jit(solution)/shard_map/ppermute | solution.py:10
  124.9 107.8 %reduce-scatter.5.cloned.1.call-start = ((), (), s32[]{:S(2)}) async-start(), calls=%async_computation.3 | async-start | bytes 1638400 | tf_op jit(solution)/shard_map/reduce_scatter | solution.py:65
  128.6 17.6 %collective-permute-start.3 = (bf16[128,5120]{1,0:T(8,128)(2,1)}, bf16[128,5120]{1,0:T(8,128)(2,1)}, u32[]{:S(2)}, u32[]{:S(2)}) collective-permute-start(bf16[128,5120]{1,0:T(8,128)(2,1)} %convolution_convert_fusion.1), channel_id=1, source_target_pairs={{4,0},{8,4},{12,8},{16,12},{20,16},{24,20},{28,24},{0,28},{5,1},{9... | collective-permute-start | bytes 3932168 | tf_op jit(solution)/shard_map/ppermute | solution.py:10
Sparse Core Ops, SparseCore 0:
  125.0 72.9 reduce-scatter.2
  200.9 31.7 reduce-scatter.4
where the time goes:
time: 241 us; the launch traced here: 240 us
  waiting for transfers between devices  184 us (76%)
  matrix products  34 us (14%)
  between operations  14.2 us (6%)
  starting transfers between devices  4.39 us (2%)
  local copies, waits for them, and re-layouts  2.97 us (1%)
    ppermute x4, waiting for transfers between devices, shifted(): return lax.ppermute(block, axis, route)  113 us
    reduce_scatter x1, waiting for transfers between devices, local(): lax.psum_scatter((gq_own + back_qkv)[None].astype(jnp.bfloat16), 'dp', sc...  38.6 us
    reduce_scatter x1, waiting for transfers between devices, local(): lax.psum_scatter((go_own + back_out)[None].astype(jnp.bfloat16), 'dp', sc...  32.4 us
    dot_general x2, matrix products, group_terms(): input_term = jnp.dot(d_qkv, w_qkv.T, preferred_element_type=jnp.float32)  8.95 us
    dot_general x2, matrix products, group_terms(): grad_wout = jnp.dot(attended.T, grad_in, preferred_element_type=jnp.float32)  7.89 us
    dot_general x2, matrix products, group_terms(): jnp.dot(inputs, w_qkv, preferred_element_type=jnp.float32)  7.43 us
  transfers between devices with their start and end apart: 6, of which 5 were waited for; matrix products, arithmetic and copies ran while one was open for 11% of the time, Pallas kernels for 0%

commit v1 on v0

v1 whole, which is shorter than its diff:
```python
import functools

import jax
import jax.numpy as jnp
from jax import lax
from jax.experimental import pallas as pl
from jax.experimental.pallas import tpu as pltpu
from jax.sharding import PartitionSpec as P

MESH = pl.DeviceIdType.MESH
F32 = jnp.float32
BF16 = jnp.bfloat16
PARTS = 2


def dot(a, b):
    return jnp.dot(a, b, preferred_element_type=F32)


def dot_nt(a, b):
    return lax.dot_general(a, b, (((1,), (1,)), ((), ())), preferred_element_type=F32)


def dot_tn(a, b):
    return lax.dot_general(a, b, (((0,), (0,)), ((), ())), preferred_element_type=F32)


def attention_terms(qkv, d_att, seg_row, head):
    scale = head ** (-0.5)
    query, keys, values = qkv[:, :head], qkv[:, head : 2 * head], qkv[:, 2 * head :]
    count = qkv.shape[0]
    seg_rows = jnp.broadcast_to(seg_row.astype(F32), (count, count))
    places = lax.broadcasted_iota(jnp.int32, (count, count), 0)
    others = lax.broadcasted_iota(jnp.int32, (count, count), 1)
    allowed = (places >= others) & (seg_rows.T == seg_rows)
    scores = jnp.where(allowed, dot_nt(query, keys) * scale, F32(-1e30))
    top = jnp.max(scores, axis=-1, keepdims=True)
    expo = jnp.where(allowed, jnp.exp(scores - top), F32(0.0))
    probs = expo / jnp.sum(expo, axis=-1, keepdims=True)
    probs_b = probs.astype(BF16)
    attended = dot(probs_b, values).astype(BF16)
    d_probs = dot_nt(d_att, values)
    d_scores = (probs * (d_probs - jnp.sum(probs * d_probs, axis=-1, keepdims=True)) * scale).astype(BF16)
    d_qkv = jnp.concatenate([dot(d_scores, keys), dot_tn(d_scores, query), dot_tn(probs_b, d_att)], axis=1)
    return d_qkv.astype(BF16), attended


def kernel(
    nb, n, wide, x_hbm, g_hbm, seg_ref, w_hbm, wo_hbm, ig_ref, gs_ref,
    x, g, xf, gf, w, wo, dt, dq, gt, from_low, from_high, term, tsend, tback,
    load_sem, out_send, out_recv, t_send, t_recv, up_send, up_recv, down_send, down_recv,
):
    b, d = lax.axis_index("blk"), lax.axis_index("dp")
    nxt, prv = lax.rem(b + 1, nb), lax.rem(b + nb - 1, nb)
    head = wo.shape[0]
    cols = 3 * head
    part = (cols + head) // PARTS

    loads = [
        pltpu.make_async_copy(src, dst, load_sem.at[i])
        for i, (src, dst) in enumerate(((x_hbm, x), (w_hbm, w), (g_hbm, g), (wo_hbm, wo)))
    ]
    for load in loads:
        load.start()

    barrier = pltpu.get_barrier_semaphore()
    for other in (nxt, prv):
        pl.semaphore_signal(barrier, inc=1, device_id={"blk": other}, device_id_type=MESH)

    @pl.when(d > 0)
    def _():
        pl.semaphore_signal(barrier, inc=1, device_id={"dp": d - 1}, device_id_type=MESH)

    @pl.when(d < n - 1)
    def _():
        pl.semaphore_signal(barrier, inc=1, device_id={"dp": d + 1}, device_id_type=MESH)

    pl.semaphore_wait(barrier, 2 + (d > 0).astype(jnp.int32) + (d < n - 1).astype(jnp.int32))

    def lanes(c):
        return pl.ds(pl.multiple_of(c * wide, 128), wide)

    def send_out(which, c):
        src, dst = ((x_hbm, xf), (g_hbm, gf))[which]
        return pltpu.make_async_remote_copy(
            src_ref=src.at[:, lanes(c)], dst_ref=dst.at[:, lanes(c)],
            send_sem=out_send.at[which, c], recv_sem=out_recv.at[which, c],
            device_id={"blk": prv}, device_id_type=MESH,
        )

    def send_term(c):
        return pltpu.make_async_remote_copy(
            src_ref=tsend.at[:, lanes(c)], dst_ref=tback.at[:, lanes(c)],
            send_sem=t_send.at[c], recv_sem=t_recv.at[c],
            device_id={"blk": nxt}, device_id_type=MESH,
        )

    def rows(p):
        return pl.ds(p * part, part)

    def send_up(k, p):
        return pltpu.make_async_remote_copy(
            src_ref=gt.at[k, rows(p)], dst_ref=from_low.at[k, rows(p)],
            send_sem=up_send.at[k, p], recv_sem=up_recv.at[k, p],
            device_id={"dp": d + 1}, device_id_type=MESH,
        )

    def send_down(k, p):
        return pltpu.make_async_remote_copy(
            src_ref=gt.at[k, rows(p)], dst_ref=from_high.at[k, rows(p)],
            send_sem=down_send.at[k, p], recv_sem=down_recv.at[k, p],
            device_id={"dp": d - 1}, device_id_type=MESH,
        )

    for which in range(2):
        for c in range(n):
            send_out(which, c).start()

    def differentiate(slot, x_ref, g_ref, wait_x, wait_g, seg_at):
        def qkv_step(c, total):
            wait_x(c)
            return total + dot(x_ref[:, lanes(c)], w[lanes(c), :])

        def att_step(c, total):
            wait_g(c)
            return total + dot_nt(g_ref[:, lanes(c)], wo[:, lanes(c)])

        count = x_ref.shape[0]
        qkv = lax.fori_loop(0, n, qkv_step, jnp.zeros((count, cols), F32)).astype(BF16)
        d_att = lax.fori_loop(0, n, att_step, jnp.zeros((count, head), F32)).astype(BF16)
        d_qkv, attended = attention_terms(qkv, d_att, seg_ref[pl.ds(seg_at, 1), :], head)
        dq[slot] = d_qkv
        dt[slot, :cols, :] = d_qkv.astype(F32).T.astype(BF16)
        dt[slot, cols:, :] = attended.astype(F32).T.astype(BF16)

    for load in loads:
        load.wait()
    differentiate(0, x, g, lambda c: None, lambda c: None, b)

    def own_term(c, carry):
        term[:, lanes(c)] = dot_nt(dq[0], w[lanes(c), :])
        return carry

    lax.fori_loop(0, n, own_term, 0)

    differentiate(
        1, xf, gf, lambda c: send_out(0, c).wait_recv(), lambda c: send_out(1, c).wait_recv(), nxt
    )

    def gradient(c, carry):
        gt[c, :cols, :] = (dot(dt[0, :cols, :], x[:, lanes(c)]) + dot(dt[1, :cols, :], xf[:, lanes(c)])).astype(BF16)
        gt[c, cols:, :] = (dot(dt[0, cols:, :], g[:, lanes(c)]) + dot(dt[1, cols:, :], gf[:, lanes(c)])).astype(BF16)
        return carry

    lax.fori_loop(0, n, gradient, 0)

    @pl.when(d == 0)
    def _():
        for k in range(n - 1, 0, -1):
            for p in range(PARTS):
                send_up(k, p).start()

    @pl.when(d == n - 1)
    def _():
        for k in range(n - 1):
            for p in range(PARTS):
                send_down(k, p).start()

    def far_term(c, carry):
        tsend[:, lanes(c)] = dot_nt(dq[1], w[lanes(c), :]).astype(BF16)
        send_term(c).start()
        return carry

    lax.fori_loop(0, n, far_term, 0)

    for j in range(n - 1):
        for p in range(PARTS):
            up, down = n - 1 - j, j

            @pl.when((d > 0) & (d < up))
            def _(up=up, p=p):
                send_up(up, p).wait_recv()
                gt[up, rows(p), :] = (gt[up, rows(p), :].astype(F32) + from_low[up, rows(p), :].astype(F32)).astype(BF16)
                send_up(up, p).start()

            @pl.when((d < n - 1) & (d > down))
            def _(down=down, p=p):
                send_down(down, p).wait_recv()
                gt[down, rows(p), :] = (
                    gt[down, rows(p), :].astype(F32) + from_high[down, rows(p), :].astype(F32)
                ).astype(BF16)
                send_down(down, p).start()

    def finish_input(c, carry):
        send_term(c).wait_recv()
        ig_ref[:, lanes(c)] = (term[:, lanes(c)] + tback[:, lanes(c)].astype(F32)).astype(BF16)
        return carry

    lax.fori_loop(0, n, finish_input, 0)

    for p in range(PARTS):

        @pl.when(d == 0)
        def _(p=p):
            send_down(d, p).wait_recv()
            gs_ref[rows(p), :] = (gt[d, rows(p), :].astype(F32) + from_high[d, rows(p), :].astype(F32)).astype(BF16)

        @pl.when(d == n - 1)
        def _(p=p):
            send_up(d, p).wait_recv()
            gs_ref[rows(p), :] = (gt[d, rows(p), :].astype(F32) + from_low[d, rows(p), :].astype(F32)).astype(BF16)

        @pl.when((d > 0) & (d < n - 1))
        def _(p=p):
            send_down(d, p).wait_recv()
            send_up(d, p).wait_recv()
            gs_ref[rows(p), :] = (
                gt[d, rows(p), :].astype(F32) + from_low[d, rows(p), :].astype(F32) + from_high[d, rows(p), :].astype(F32)
            ).astype(BF16)

    for c in range(n):
        send_out(0, c).wait_send()
        send_out(1, c).wait_send()
        send_term(c).wait_send()
        for p in range(PARTS):

            @pl.when(d < c)
            def _(c=c, p=p):
                send_up(c, p).wait_send()

            @pl.when(d > c)
            def _(c=c, p=p):
                send_down(c, p).wait_send()


def spread(array, dim, n, wide):
    shape = array.shape
    each = shape[dim] // n
    if each == wide:
        return array
    split = array.reshape(shape[:dim] + (n, each) + shape[dim + 1 :])
    pads = [(0, 0)] * split.ndim
    pads[dim + 1] = (0, wide - each)
    return jnp.pad(split, pads).reshape(shape[:dim] + (n * wide,) + shape[dim + 1 :])


def local(normed_input, segment_ids, weights_qkv, weights_out, cotangent):
    nb, n = lax.axis_size("blk"), lax.axis_size("dp")
    _, count, depth = normed_input.shape
    head = weights_out.shape[1]
    each = depth // n
    wide = -(-each // 128) * 128
    full = n * wide
    rows = 4 * head
    hbm = pl.BlockSpec(memory_space=pl.ANY)
    vmem = pl.BlockSpec(memory_space=pltpu.VMEM)
    dma = pltpu.SemaphoreType.DMA
    seq = pltpu.VMEM((count, full), BF16)
    shards = pltpu.VMEM((n, rows, wide), BF16)
    input_grad, summed = pl.pallas_call(
        functools.partial(kernel, nb, n, wide),
        out_shape=(jax.ShapeDtypeStruct((count, full), BF16), jax.ShapeDtypeStruct((rows, wide), BF16)),
        in_specs=[hbm, hbm, vmem, hbm, hbm],
        out_specs=(vmem, vmem),
        scratch_shapes=[
            seq, seq, seq, seq,
            pltpu.VMEM((full, 3 * head), BF16),
            pltpu.VMEM((head, full), BF16),
            pltpu.VMEM((2, rows, count), BF16),
            pltpu.VMEM((2, count, 3 * head), BF16),
            shards, shards, shards,
            pltpu.VMEM((count, full), F32),
            seq, seq,
            dma((4,)), dma((2, n)), dma((2, n)), dma((n,)), dma((n,)),
            dma((n, PARTS)), dma((n, PARTS)), dma((n, PARTS)), dma((n, PARTS)),
        ],
        compiler_params=pltpu.CompilerParams(
            collective_id=0, has_side_effects=True, vmem_limit_bytes=60 * 1024 * 1024
        ),
    )(
        spread(normed_input[0], 1, n, wide),
        spread(cotangent[0], 1, n, wide),
        segment_ids[0],
        spread(weights_qkv[0], 0, n, wide),
        spread(weights_out[0], 1, n, wide),
    )
    if each != wide:
        input_grad = input_grad.reshape(count, n, wide)[:, :, :each].reshape(count, depth)
        summed = summed[:, :each]
    return input_grad[None], summed[: 3 * head].T[None], summed[3 * head :][None]


def solution(mesh):
    placed = (
        P(("blk", "dp"), None, None),
        P("dp", None, None),
        P("blk", None, None),
        P("blk", None, None),
        P(("blk", "dp"), None, None),
    )
    return jax.shard_map(
        local,
        mesh=mesh,
        in_specs=placed,
        out_specs=(P(("blk", "dp"), None, None), P("blk", "dp", None), P("blk", None, "dp")),
        check_vma=False,
    )
```

time: 241 us -> 145 us (0.60)
  the two profiles are of different devices: /device:TPU:1 before, /device:TPU:19 now
where the time goes in v1:
time: 145 us
  Pallas kernels  136 us (94%)
  local copies, waits for them, and re-layouts  7.7 us (5%)
    pallas_call x1, Pallas kernels, local(): pl.pallas_call(functools.partial(kernel, nb, n, wide), out_shape=(jax.Sha...  136 us
    unnamed x2, local copies, waits for them, and re-layouts  4.71 us

profile of v1, /device:TPU:19, one launch (start us, length us, event | category | flops | bytes accessed | tf_op | source)
XLA Modules:
  0.0 144.8 jit_solution(7679385473544829916)
XLA Ops:
  0.6 136.4 %shard_map.76 = (bf16[256,5120]{1,0:T(8,128)(2,1)}, bf16[512,1280]{1,0:T(8,128)(2,1)}) custom-call(bf16[256,5120]{1,0:T(8,128)(2,1)} %bitcast.14, bf16[256,5120]{1,0:T(8,128)(2,1)} %bitcast.15, s32[8,256]{1,0:T(8,128)} %bitcast.17, bf16[5120,384]{1,0:T(8,128)(2,1)} %bitcast.12, bf16[128,5120]{1,0:T(8,128)(2,1)} %bitcast.16), custom_call_target="tpu_custom_call" | custom-call | tf_op jit(solution)/shard_map/pallas_call | solution.py:260
  137.1 1.7 %slice_bitcast_fusion.1 = bf16[1,128,1280]{2,1,0:T(8,128)(2,1)} fusion(bf16[512,1280]{1,0:T(8,128)(2,1)} %get-tuple-element.6), kind=kLoop, calls=%fused_computation.1 | loop fusion | bytes 655360 | tf_op jit(solution)/shard_map/broadcast_in_dim | solution.py:290
  138.8 1.3 slice_bitcast_fusion
  140.1 1.3 copy.8
  141.4 3.4 %copy.10 = bf16[1,256,5120]{2,1,0:T(8,128)(2,1)} copy(bf16[1,256,5120]{2,1,0:T(8,128)(2,1)} %bitcast.13) | data formatting | bytes 5242880

commit v2 on v1

--- a/solution.py
+++ b/solution.py
@@ -10,7 +10,7 @@
 MESH = pl.DeviceIdType.MESH
 F32 = jnp.float32
 BF16 = jnp.bfloat16
-PARTS = 2
+PARTS = 4
 
 
 def dot(a, b):
@@ -46,19 +46,21 @@
 
 
 def kernel(
-    nb, n, wide, x_hbm, g_hbm, seg_ref, w_hbm, wo_hbm, ig_ref, gs_ref,
-    x, g, xf, gf, w, wo, dt, dq, gt, from_low, from_high, term, tsend, tback,
-    load_sem, out_send, out_recv, t_send, t_recv, up_send, up_recv, down_send, down_recv,
+    nb, n, wide, x_hbm, g_hbm, seg_ref, w_hbm, wo_hbm, ig_hbm, gs_ref,
+    xx, gg, w, wo, dt, dq, gt, from_low, from_high, term, tsend, tback,
+    load_sem, out_send, out_recv, t_send, t_recv, up_send, up_recv, down_send, down_recv, store_sem,
 ):
     b, d = lax.axis_index("blk"), lax.axis_index("dp")
     nxt, prv = lax.rem(b + 1, nb), lax.rem(b + nb - 1, nb)
     head = wo.shape[0]
     cols = 3 * head
+    count = tsend.shape[0]
     part = (cols + head) // PARTS
+    own, far = pl.ds(0, count), pl.ds(count, count)
 
     loads = [
         pltpu.make_async_copy(src, dst, load_sem.at[i])
-        for i, (src, dst) in enumerate(((x_hbm, x), (w_hbm, w), (g_hbm, g), (wo_hbm, wo)))
+        for i, (src, dst) in enumerate(((x_hbm, xx.at[own]), (w_hbm, w), (g_hbm, gg.at[own]), (wo_hbm, wo)))
     ]
     for load in loads:
         load.start()
@@ -81,9 +83,9 @@
         return pl.ds(pl.multiple_of(c * wide, 128), wide)
 
     def send_out(which, c):
-        src, dst = ((x_hbm, xf), (g_hbm, gf))[which]
+        src, dst = ((x_hbm, xx), (g_hbm, gg))[which]
         return pltpu.make_async_remote_copy(
-            src_ref=src.at[:, lanes(c)], dst_ref=dst.at[:, lanes(c)],
+            src_ref=src.at[:, lanes(c)], dst_ref=dst.at[far, lanes(c)],
             send_sem=out_send.at[which, c], recv_sem=out_recv.at[which, c],
             device_id={"blk": prv}, device_id_type=MESH,
         )
@@ -96,7 +98,7 @@
         )
 
     def rows(p):
-        return pl.ds(p * part, part)
+        return pl.ds(pl.multiple_of(p * part, part), part)
 
     def send_up(k, p):
         return pltpu.make_async_remote_copy(
@@ -116,26 +118,25 @@
         for c in range(n):
             send_out(which, c).start()
 
-    def differentiate(slot, x_ref, g_ref, wait_x, wait_g, seg_at):
+    def differentiate(slot, at, wait_x, wait_g, seg_at):
         def qkv_step(c, total):
             wait_x(c)
-            return total + dot(x_ref[:, lanes(c)], w[lanes(c), :])
+            return total + dot(xx[at, lanes(c)], w[lanes(c), :])
 
         def att_step(c, total):
             wait_g(c)
-            return total + dot_nt(g_ref[:, lanes(c)], wo[:, lanes(c)])
-
-        count = x_ref.shape[0]
+            return total + dot_nt(gg[at, lanes(c)], wo[:, lanes(c)])
+
         qkv = lax.fori_loop(0, n, qkv_step, jnp.zeros((count, cols), F32)).astype(BF16)
         d_att = lax.fori_loop(0, n, att_step, jnp.zeros((count, head), F32)).astype(BF16)
         d_qkv, attended = attention_terms(qkv, d_att, seg_ref[pl.ds(seg_at, 1), :], head)
         dq[slot] = d_qkv
-        dt[slot, :cols, :] = d_qkv.astype(F32).T.astype(BF16)
-        dt[slot, cols:, :] = attended.astype(F32).T.astype(BF16)
+        dt[:cols, at] = d_qkv.astype(F32).T.astype(BF16)
+        dt[cols:, at] = attended.astype(F32).T.astype(BF16)
 
     for load in loads:
         load.wait()
-    differentiate(0, x, g, lambda c: None, lambda c: None, b)
+    differentiate(0, own, lambda c: None, lambda c: None, b)
 
     def own_term(c, carry):
         term[:, lanes(c)] = dot_nt(dq[0], w[lanes(c), :])
@@ -143,28 +144,26 @@
 
     lax.fori_loop(0, n, own_term, 0)
 
-    differentiate(
-        1, xf, gf, lambda c: send_out(0, c).wait_recv(), lambda c: send_out(1, c).wait_recv(), nxt
-    )
-
-    def gradient(c, carry):
-        gt[c, :cols, :] = (dot(dt[0, :cols, :], x[:, lanes(c)]) + dot(dt[1, :cols, :], xf[:, lanes(c)])).astype(BF16)
-        gt[c, cols:, :] = (dot(dt[0, cols:, :], g[:, lanes(c)]) + dot(dt[1, cols:, :], gf[:, lanes(c)])).astype(BF16)
-        return carry
-
-    lax.fori_loop(0, n, gradient, 0)
-
-    @pl.when(d == 0)
-    def _():
-        for k in range(n - 1, 0, -1):
+    differentiate(1, far, lambda c: send_out(0, c).wait_recv(), lambda c: send_out(1, c).wait_recv(), nxt)
+
+    def gradient(i, carry):
+        k = jnp.where(d == n - 1, i, n - 1 - i)
+        gt[k, :cols, :] = dot(dt[:cols, :], xx[:, lanes(k)]).astype(BF16)
+        gt[k, cols:, :] = dot(dt[cols:, :], gg[:, lanes(k)]).astype(BF16)
+
+        @pl.when((d == 0) & (k > 0))
+        def _():
             for p in range(PARTS):
                 send_up(k, p).start()
 
-    @pl.when(d == n - 1)
-    def _():
-        for k in range(n - 1):
+        @pl.when((d == n - 1) & (k < n - 1))
+        def _():
             for p in range(PARTS):
                 send_down(k, p).start()
+
+        return carry
+
+    lax.fori_loop(0, n, gradient, 0)
 
     def far_term(c, carry):
         tsend[:, lanes(c)] = dot_nt(dq[1], w[lanes(c), :]).astype(BF16)
@@ -173,27 +172,34 @@
 
     lax.fori_loop(0, n, far_term, 0)
 
-    for j in range(n - 1):
-        for p in range(PARTS):
-            up, down = n - 1 - j, j
-
-            @pl.when((d > 0) & (d < up))
-            def _(up=up, p=p):
-                send_up(up, p).wait_recv()
-                gt[up, rows(p), :] = (gt[up, rows(p), :].astype(F32) + from_low[up, rows(p), :].astype(F32)).astype(BF16)
-                send_up(up, p).start()
-
-            @pl.when((d < n - 1) & (d > down))
-            def _(down=down, p=p):
-                send_down(down, p).wait_recv()
-                gt[down, rows(p), :] = (
-                    gt[down, rows(p), :].astype(F32) + from_high[down, rows(p), :].astype(F32)
-                ).astype(BF16)
-                send_down(down, p).start()
+    def tick(t, carry):
+        up, down = t - d, t - (n - 1 - d)
+
+        @pl.when((d > 0) & (up >= 0) & (up < (n - 1 - d) * PARTS))
+        def _():
+            k, p = n - 1 - up // PARTS, up % PARTS
+            send_up(k, p).wait_recv()
+            gt[k, rows(p), :] = (gt[k, rows(p), :].astype(F32) + from_low[k, rows(p), :].astype(F32)).astype(BF16)
+            send_up(k, p).start()
+
+        @pl.when((d < n - 1) & (down >= 0) & (down < d * PARTS))
+        def _():
+            k, p = down // PARTS, down % PARTS
+            send_down(k, p).wait_recv()
+            gt[k, rows(p), :] = (gt[k, rows(p), :].astype(F32) + from_high[k, rows(p), :].astype(F32)).astype(BF16)
+            send_down(k, p).start()
+
+        return carry
+
+    lax.fori_loop(1, 1 + (n - 2) * PARTS, tick, 0)
+
+    def store(c):
+        return pltpu.make_async_copy(tback.at[:, lanes(c)], ig_hbm.at[:, lanes(c)], store_sem.at[c])
 
     def finish_input(c, carry):
         send_term(c).wait_recv()
-        ig_ref[:, lanes(c)] = (term[:, lanes(c)] + tback[:, lanes(c)].astype(F32)).astype(BF16)
+        tback[:, lanes(c)] = (term[:, lanes(c)] + tback[:, lanes(c)].astype(F32)).astype(BF16)
+        store(c).start()
         return carry
 
     lax.fori_loop(0, n, finish_input, 0)
@@ -222,6 +228,7 @@
         send_out(0, c).wait_send()
         send_out(1, c).wait_send()
         send_term(c).wait_send()
+        store(c).wait()
         for p in range(PARTS):
 
             @pl.when(d < c)
@@ -231,6 +238,33 @@
             @pl.when(d > c)
             def _(c=c, p=p):
                 send_down(c, p).wait_send()
+
+
+def place_kernel(n, wide, ig_hbm, gs_hbm, out_ig, out_qkv, out_out, shard, turned, ig, sem):
+    cols = turned.shape[1]
+
+    def lanes(c):
+        return pl.ds(c * wide, wide)
+
+    fetch = pltpu.make_async_copy(gs_hbm, shard, sem.at[0])
+    fetch.start()
+    reads = [pltpu.make_async_copy(ig_hbm.at[:, lanes(c)], ig.at[:, lanes(c)], sem.at[3 + c]) for c in range(n)]
+    writes = [pltpu.make_async_copy(ig.at[:, lanes(c)], out_ig.at[:, lanes(c)], sem.at[3 + n + c]) for c in range(n)]
+    for read in reads:
+        read.start()
+    fetch.wait()
+    plain = pltpu.make_async_copy(shard.at[pl.ds(cols, shard.shape[0] - cols)], out_out, sem.at[1])
+    plain.start()
+    for read, write in zip(reads, writes):
+        read.wait()
+        write.start()
+    turned[...] = shard[:cols, :].astype(F32).T.astype(BF16)
+    across = pltpu.make_async_copy(turned, out_qkv, sem.at[2])
+    across.start()
+    plain.wait()
+    across.wait()
+    for write in writes:
+        write.wait()
 
 
 def spread(array, dim, n, wide):
@@ -256,23 +290,24 @@
     vmem = pl.BlockSpec(memory_space=pltpu.VMEM)
     dma = pltpu.SemaphoreType.DMA
     seq = pltpu.VMEM((count, full), BF16)
+    pairs = pltpu.VMEM((2 * count, full), BF16)
     shards = pltpu.VMEM((n, rows, wide), BF16)
     input_grad, summed = pl.pallas_call(
         functools.partial(kernel, nb, n, wide),
         out_shape=(jax.ShapeDtypeStruct((count, full), BF16), jax.ShapeDtypeStruct((rows, wide), BF16)),
         in_specs=[hbm, hbm, vmem, hbm, hbm],
-        out_specs=(vmem, vmem),
+        out_specs=(hbm, vmem),
         scratch_shapes=[
-            seq, seq, seq, seq,
+            pairs, pairs,
             pltpu.VMEM((full, 3 * head), BF16),
             pltpu.VMEM((head, full), BF16),
-            pltpu.VMEM((2, rows, count), BF16),
+            pltpu.VMEM((rows, 2 * count), BF16),
             pltpu.VMEM((2, count, 3 * head), BF16),
             shards, shards, shards,
             pltpu.VMEM((count, full), F32),
             seq, seq,
             dma((4,)), dma((2, n)), dma((2, n)), dma((n,)), dma((n,)),
-            dma((n, PARTS)), dma((n, PARTS)), dma((n, PARTS)), dma((n, PARTS)),
+            dma((n, PARTS)), dma((n, PARTS)), dma((n, PARTS)), dma((n, PARTS)), dma((n,)),
         ],
         compiler_params=pltpu.CompilerParams(
             collective_id=0, has_side_effects=True, vmem_limit_bytes=60 * 1024 * 1024
@@ -284,10 +319,26 @@
         spread(weights_qkv[0], 0, n, wide),
         spread(weights_out[0], 1, n, wide),
     )
+    input_grad, grad_qkv, grad_out = pl.pallas_call(
+        functools.partial(place_kernel, n, wide),
+        out_shape=(
+            jax.ShapeDtypeStruct((count, full), BF16),
+            jax.ShapeDtypeStruct((wide, 3 * head), BF16),
+            jax.ShapeDtypeStruct((head, wide), BF16),
+        ),
+        in_specs=[hbm, hbm],
+        out_specs=(hbm, hbm, hbm),
+        scratch_shapes=[
+            pltpu.VMEM((rows, wide), BF16),
+            pltpu.VMEM((wide, 3 * head), BF16),
+            pltpu.VMEM((count, full), BF16),
+            dma((3 + 2 * n,)),
+        ],
+        compiler_params=pltpu.CompilerParams(vmem_limit_bytes=60 * 1024 * 1024),
+    )(input_grad, summed)
     if each != wide:
         input_grad = input_grad.reshape(count, n, wide)[:, :, :each].reshape(count, depth)
-        summed = summed[:, :each]
-    return input_grad[None], summed[: 3 * head].T[None], summed[3 * head :][None]
+    return input_grad[None], grad_qkv[None, :each], grad_out[None, :, :each]
 
 
 def solution(mesh):

time: 145 us -> 114 us (0.79)
  the two profiles are of different devices: /device:TPU:19 before, /device:TPU:1 now
where the time goes in v2:
time: 114 us
  Pallas kernels  113 us (99%)
    pallas_call x1, Pallas kernels, local(): pl.pallas_call(functools.partial(kernel, nb, n, wide), out_shape=(jax.Sha...  109 us
    pallas_call x1, Pallas kernels, local(): pl.pallas_call(functools.partial(place_kernel, n, wide), out_shape=(jax.S...  3.47 us

profile of v2, /device:TPU:1, one launch (start us, length us, event | category | flops | bytes accessed | tf_op | source)
XLA Modules:
  0.0 113.5 jit_solution(1572822546646479894)
XLA Ops:
  0.6 109.4 %shard_map.76 = (bf16[256,5120]{1,0:T(8,128)(2,1)}, bf16[512,1280]{1,0:T(8,128)(2,1)}) custom-call(bf16[256,5120]{1,0:T(8,128)(2,1)} %bitcast.9, bf16[256,5120]{1,0:T(8,128)(2,1)} %bitcast.10, s32[8,256]{1,0:T(8,128)} %bitcast.12, bf16[5120,384]{1,0:T(8,128)(2,1)} %bitcast.8, bf16[128,5120]{1,0:T(8,128)(2,1)} %bitcast.11), custom_call_target="tpu_custom_call" | custom-call | tf_op jit(solution)/shard_map/pallas_call | solution.py:295
  110.1 3.5 %shard_map.77 = (bf16[256,5120]{1,0:T(8,128)(2,1)}, bf16[1280,384]{1,0:T(8,128)(2,1)}, bf16[128,1280]{1,0:T(8,128)(2,1)}) custom-call(bf16[256,5120]{1,0:T(8,128)(2,1)} %get-tuple-element.8.ig_hbm, bf16[512,1280]{1,0:T(8,128)(2,1)} %get-tuple-element.9.gs_hbm), custom_call_target="tpu_custom_call" | custom-call | tf_op jit(solution)/shard_map/pallas_call | solution.py:322

commit v3 on v2

--- a/solution.py
+++ b/solution.py
@@ -25,7 +25,7 @@
     return lax.dot_general(a, b, (((0,), (0,)), ((), ())), preferred_element_type=F32)
 
 
-def attention_terms(qkv, d_att, seg_row, head):
+def attention_terms(qkv, d_att_of, seg_row, head):
     scale = head ** (-0.5)
     query, keys, values = qkv[:, :head], qkv[:, head : 2 * head], qkv[:, 2 * head :]
     count = qkv.shape[0]
@@ -39,6 +39,7 @@
     probs = expo / jnp.sum(expo, axis=-1, keepdims=True)
     probs_b = probs.astype(BF16)
     attended = dot(probs_b, values).astype(BF16)
+    d_att = d_att_of()
     d_probs = dot_nt(d_att, values)
     d_scores = (probs * (d_probs - jnp.sum(probs * d_probs, axis=-1, keepdims=True)) * scale).astype(BF16)
     d_qkv = jnp.concatenate([dot(d_scores, keys), dot_tn(d_scores, query), dot_tn(probs_b, d_att)], axis=1)
@@ -46,7 +47,7 @@
 
 
 def kernel(
-    nb, n, wide, x_hbm, g_hbm, seg_ref, w_hbm, wo_hbm, ig_hbm, gs_ref,
+    nb, n, wide, x_hbm, g_hbm, seg_ref, w_hbm, wo_hbm, ig_hbm, turned, plain,
     xx, gg, w, wo, dt, dq, gt, from_low, from_high, term, tsend, tback,
     load_sem, out_send, out_recv, t_send, t_recv, up_send, up_recv, down_send, down_recv, store_sem,
 ):
@@ -55,7 +56,7 @@
     head = wo.shape[0]
     cols = 3 * head
     count = tsend.shape[0]
-    part = (cols + head) // PARTS
+    part = head
     own, far = pl.ds(0, count), pl.ds(count, count)
 
     loads = [
@@ -128,8 +129,11 @@
             return total + dot_nt(gg[at, lanes(c)], wo[:, lanes(c)])
 
         qkv = lax.fori_loop(0, n, qkv_step, jnp.zeros((count, cols), F32)).astype(BF16)
-        d_att = lax.fori_loop(0, n, att_step, jnp.zeros((count, head), F32)).astype(BF16)
-        d_qkv, attended = attention_terms(qkv, d_att, seg_ref[pl.ds(seg_at, 1), :], head)
+
+        def d_att_of():
+            return lax.fori_loop(0, n, att_step, jnp.zeros((count, head), F32)).astype(BF16)
+
+        d_qkv, attended = attention_terms(qkv, d_att_of, seg_ref[pl.ds(seg_at, 1), :], head)
         dq[slot] = d_qkv
         dt[:cols, at] = d_qkv.astype(F32).T.astype(BF16)
         dt[cols:, at] = attended.astype(F32).T.astype(BF16)
@@ -137,12 +141,6 @@
     for load in loads:
         load.wait()
     differentiate(0, own, lambda c: None, lambda c: None, b)
-
-    def own_term(c, carry):
-        term[:, lanes(c)] = dot_nt(dq[0], w[lanes(c), :])
-        return carry
-
-    lax.fori_loop(0, n, own_term, 0)
 
     differentiate(1, far, lambda c: send_out(0, c).wait_recv(), lambda c: send_out(1, c).wait_recv(), nxt)
 
@@ -193,6 +191,12 @@
 
     lax.fori_loop(1, 1 + (n - 2) * PARTS, tick, 0)
 
+    def own_term(c, carry):
+        term[:, lanes(c)] = dot_nt(dq[0], w[lanes(c), :])
+        return carry
+
+    lax.fori_loop(0, n, own_term, 0)
+
     def store(c):
         return pltpu.make_async_copy(tback.at[:, lanes(c)], ig_hbm.at[:, lanes(c)], store_sem.at[c])
 
@@ -205,24 +209,15 @@
     lax.fori_loop(0, n, finish_input, 0)
 
     for p in range(PARTS):
-
-        @pl.when(d == 0)
-        def _(p=p):
-            send_down(d, p).wait_recv()
-            gs_ref[rows(p), :] = (gt[d, rows(p), :].astype(F32) + from_high[d, rows(p), :].astype(F32)).astype(BF16)
-
-        @pl.when(d == n - 1)
-        def _(p=p):
-            send_up(d, p).wait_recv()
-            gs_ref[rows(p), :] = (gt[d, rows(p), :].astype(F32) + from_low[d, rows(p), :].astype(F32)).astype(BF16)
-
-        @pl.when((d > 0) & (d < n - 1))
-        def _(p=p):
-            send_down(d, p).wait_recv()
-            send_up(d, p).wait_recv()
-            gs_ref[rows(p), :] = (
-                gt[d, rows(p), :].astype(F32) + from_low[d, rows(p), :].astype(F32) + from_high[d, rows(p), :].astype(F32)
-            ).astype(BF16)
+        pl.when(d > 0)(lambda p=p: send_up(d, p).wait_recv())
+        pl.when(d < n - 1)(lambda p=p: send_down(d, p).wait_recv())
+        total = gt[d, rows(p), :].astype(F32)
+        total += jnp.where(d > 0, from_low[d, rows(p), :].astype(F32), F32(0.0))
+        total += jnp.where(d < n - 1, from_high[d, rows(p), :].astype(F32), F32(0.0))
+        if p < PARTS - 1:
+            turned[:, rows(p)] = total.T.astype(BF16)
+        else:
+            plain[...] = total.astype(BF16)
 
     for c in range(n):
         send_out(0, c).wait_send()
@@ -240,29 +235,19 @@
                 send_down(c, p).wait_send()
 
 
-def place_kernel(n, wide, ig_hbm, gs_hbm, out_ig, out_qkv, out_out, shard, turned, ig, sem):
-    cols = turned.shape[1]
-
+def place_kernel(n, wide, ig_hbm, qkv_hbm, out_hbm, ig_to, qkv_to, out_to, ig, qkv, out, sem):
     def lanes(c):
         return pl.ds(c * wide, wide)
 
-    fetch = pltpu.make_async_copy(gs_hbm, shard, sem.at[0])
-    fetch.start()
-    reads = [pltpu.make_async_copy(ig_hbm.at[:, lanes(c)], ig.at[:, lanes(c)], sem.at[3 + c]) for c in range(n)]
-    writes = [pltpu.make_async_copy(ig.at[:, lanes(c)], out_ig.at[:, lanes(c)], sem.at[3 + n + c]) for c in range(n)]
+    legs = [(ig_hbm.at[:, lanes(c)], ig.at[:, lanes(c)], ig_to.at[:, lanes(c)]) for c in range(n)]
+    legs += [(qkv_hbm, qkv, qkv_to), (out_hbm, out, out_to)]
+    reads = [pltpu.make_async_copy(src, mid, sem.at[0, i]) for i, (src, mid, _) in enumerate(legs)]
+    writes = [pltpu.make_async_copy(mid, dst, sem.at[1, i]) for i, (_, mid, dst) in enumerate(legs)]
     for read in reads:
         read.start()
-    fetch.wait()
-    plain = pltpu.make_async_copy(shard.at[pl.ds(cols, shard.shape[0] - cols)], out_out, sem.at[1])
-    plain.start()
     for read, write in zip(reads, writes):
         read.wait()
         write.start()
-    turned[...] = shard[:cols, :].astype(F32).T.astype(BF16)
-    across = pltpu.make_async_copy(turned, out_qkv, sem.at[2])
-    across.start()
-    plain.wait()
-    across.wait()
     for write in writes:
         write.wait()
 
@@ -292,11 +277,16 @@
     seq = pltpu.VMEM((count, full), BF16)
     pairs = pltpu.VMEM((2 * count, full), BF16)
     shards = pltpu.VMEM((n, rows, wide), BF16)
-    input_grad, summed = pl.pallas_call(
+    results = (
+        jax.ShapeDtypeStruct((count, full), BF16),
+        jax.ShapeDtypeStruct((wide, 3 * head), BF16),
+        jax.ShapeDtypeStruct((head, wide), BF16),
+    )
+    made = pl.pallas_call(
         functools.partial(kernel, nb, n, wide),
-        out_shape=(jax.ShapeDtypeStruct((count, full), BF16), jax.ShapeDtypeStruct((rows, wide), BF16)),
+        out_shape=results,
         in_specs=[hbm, hbm, vmem, hbm, hbm],
-        out_specs=(hbm, vmem),
+        out_specs=(hbm, vmem, vmem),
         scratch_shapes=[
             pairs, pairs,
             pltpu.VMEM((full, 3 * head), BF16),
@@ -321,21 +311,12 @@
     )
     input_grad, grad_qkv, grad_out = pl.pallas_call(
         functools.partial(place_kernel, n, wide),
-        out_shape=(
-            jax.ShapeDtypeStruct((count, full), BF16),
-            jax.ShapeDtypeStruct((wide, 3 * head), BF16),
-            jax.ShapeDtypeStruct((head, wide), BF16),
-        ),
-        in_specs=[hbm, hbm],
+        out_shape=results,
+        in_specs=[hbm, hbm, hbm],
         out_specs=(hbm, hbm, hbm),
-        scratch_shapes=[
-            pltpu.VMEM((rows, wide), BF16),
-            pltpu.VMEM((wide, 3 * head), BF16),
-            pltpu.VMEM((count, full), BF16),
-            dma((3 + 2 * n,)),
-        ],
+        scratch_shapes=[pltpu.VMEM(made_one.shape, BF16) for made_one in results] + [dma((2, n + 2))],
         compiler_params=pltpu.CompilerParams(vmem_limit_bytes=60 * 1024 * 1024),
-    )(input_grad, summed)
+    )(*made)
     if each != wide:
         input_grad = input_grad.reshape(count, n, wide)[:, :, :each].reshape(count, depth)
     return input_grad[None], grad_qkv[None, :each], grad_out[None, :, :each]

time: 114 us -> 113 us (level)
  no operation moved by 1% of the time
where the time goes in v3:
time: 113 us
  Pallas kernels  112 us (99%)
    pallas_call x1, Pallas kernels, local(): pl.pallas_call(functools.partial(kernel, nb, n, wide), out_shape=results,...  109 us
    pallas_call x1, Pallas kernels, local(): pl.pallas_call(functools.partial(place_kernel, n, wide), out_shape=result...  3.16 us

profile of v3, /device:TPU:1, one launch (start us, length us, event | category | flops | bytes accessed | tf_op | source)
XLA Modules:
  0.0 112.8 jit_solution(14658228306732972585)
XLA Ops:
  0.6 109.0 %shard_map.76 = (bf16[256,5120]{1,0:T(8,128)(2,1)}, bf16[1280,384]{1,0:T(8,128)(2,1)}, bf16[128,1280]{1,0:T(8,128)(2,1)}) custom-call(bf16[256,5120]{1,0:T(8,128)(2,1)} %bitcast.9, bf16[256,5120]{1,0:T(8,128)(2,1)} %bitcast.10, s32[8,256]{1,0:T(8,128)} %bitcast.12, bf16[5120,384]{1,0:T(8,128)(2,1)} %bitcast.8, bf16[128,5120]{1,0:T(8,128)(2,1)} %bitcast.11), custom_call_target="tpu_custom_call" | custom-call | tf_op jit(solution)/shard_map/pallas_call | solution.py:285
  109.6 3.2 %shard_map.77 = (bf16[256,5120]{1,0:T(8,128)(2,1)}, bf16[1280,384]{1,0:T(8,128)(2,1)}, bf16[128,1280]{1,0:T(8,128)(2,1)}) custom-call(bf16[256,5120]{1,0:T(8,128)(2,1)} %get-tuple-element.9.ig_hbm, bf16[1280,384]{1,0:T(8,128)(2,1)} %get-tuple-element.10.qkv_hbm, bf16[128,1280]{1,0:T(8,128)(2,1)} %get-tuple-element.11.out_hbm), custom_call_target="tpu_custom_call" | custom-call | tf_op jit(solution)/shard_map/pallas_call | solution.py:312

commit v4 on v3

--- a/solution.py
+++ b/solution.py
@@ -48,8 +48,8 @@
 
 def kernel(
     nb, n, wide, x_hbm, g_hbm, seg_ref, w_hbm, wo_hbm, ig_hbm, turned, plain,
-    xx, gg, w, wo, dt, dq, gt, from_low, from_high, term, tsend, tback,
-    load_sem, out_send, out_recv, t_send, t_recv, up_send, up_recv, down_send, down_recv, store_sem,
+    xx, gg, w, wo, wo_prev, go_to, go_from, att_to, att_from, back_to, back_from, turned_att, dt, dq, gt, from_low, from_high, term, tsend, tback,
+    load_sem, x_send, x_recv, go_send, go_recv, wo_sem, att_sem, back_sem, t_send, t_recv, up_send, up_recv, down_send, down_recv, store_sem,
 ):
     b, d = lax.axis_index("blk"), lax.axis_index("dp")
     nxt, prv = lax.rem(b + 1, nb), lax.rem(b + nb - 1, nb)
@@ -61,7 +61,7 @@
 
     loads = [
         pltpu.make_async_copy(src, dst, load_sem.at[i])
-        for i, (src, dst) in enumerate(((x_hbm, xx.at[own]), (w_hbm, w), (g_hbm, gg.at[own]), (wo_hbm, wo)))
+        for i, (src, dst) in enumerate(((x_hbm, xx.at[own]), (w_hbm, w), (g_hbm, gg), (wo_hbm, wo)))
     ]
     for load in loads:
         load.start()
@@ -83,11 +83,17 @@
     def lanes(c):
         return pl.ds(pl.multiple_of(c * wide, 128), wide)
 
-    def send_out(which, c):
-        src, dst = ((x_hbm, xx), (g_hbm, gg))[which]
+    def send_x(c):
         return pltpu.make_async_remote_copy(
-            src_ref=src.at[:, lanes(c)], dst_ref=dst.at[far, lanes(c)],
-            send_sem=out_send.at[which, c], recv_sem=out_recv.at[which, c],
+            src_ref=x_hbm.at[:, lanes(c)], dst_ref=xx.at[far, lanes(c)],
+            send_sem=x_send.at[c], recv_sem=x_recv.at[c],
+            device_id={"blk": prv}, device_id_type=MESH,
+        )
+
+    def send_go(c):
+        return pltpu.make_async_remote_copy(
+            src_ref=go_to.at[:, lanes(c)], dst_ref=go_from.at[:, lanes(c)],
+            send_sem=go_send.at[c], recv_sem=go_recv.at[c],
             device_id={"blk": prv}, device_id_type=MESH,
         )
 
@@ -115,53 +121,102 @@
             device_id={"dp": d - 1}, device_id_type=MESH,
         )
 
-    for which in range(2):
+    send_wo = pltpu.make_async_remote_copy(
+        src_ref=wo_hbm, dst_ref=wo_prev, send_sem=wo_sem.at[0], recv_sem=wo_sem.at[1],
+        device_id={"blk": nxt}, device_id_type=MESH,
+    )
+    send_att = pltpu.make_async_remote_copy(
+        src_ref=att_to, dst_ref=att_from, send_sem=att_sem.at[0], recv_sem=att_sem.at[1],
+        device_id={"blk": prv}, device_id_type=MESH,
+    )
+    send_back = pltpu.make_async_remote_copy(
+        src_ref=back_to, dst_ref=back_from, send_sem=back_sem.at[0], recv_sem=back_sem.at[1],
+        device_id={"blk": nxt}, device_id_type=MESH,
+    )
+    odd = lax.rem(b, 2) == 1
+    even = lax.rem(b, 2) == 0
+
+    def start_x():
         for c in range(n):
-            send_out(which, c).start()
-
-    def differentiate(slot, at, wait_x, wait_g, seg_at):
-        def qkv_step(c, total):
+            send_x(c).start()
+
+    send_wo.start()
+
+    pl.when(odd)(start_x)
+
+    def project(at, wait_x):
+        def step(c, total):
             wait_x(c)
             return total + dot(xx[at, lanes(c)], w[lanes(c), :])
 
-        def att_step(c, total):
-            wait_g(c)
-            return total + dot_nt(gg[at, lanes(c)], wo[:, lanes(c)])
-
-        qkv = lax.fori_loop(0, n, qkv_step, jnp.zeros((count, cols), F32)).astype(BF16)
-
-        def d_att_of():
-            return lax.fori_loop(0, n, att_step, jnp.zeros((count, head), F32)).astype(BF16)
-
+        return lax.fori_loop(0, n, step, jnp.zeros((count, cols), F32)).astype(BF16)
+
+    def att_grad(weights):
+        def step(c, total):
+            return total + dot_nt(gg[:, lanes(c)], weights[:, lanes(c)])
+
+        return lax.fori_loop(0, n, step, jnp.zeros((count, head), F32)).astype(BF16)
+
+    def differentiate(slot, at, qkv, d_att_of, seg_at):
         d_qkv, attended = attention_terms(qkv, d_att_of, seg_ref[pl.ds(seg_at, 1), :], head)
         dq[slot] = d_qkv
-        dt[:cols, at] = d_qkv.astype(F32).T.astype(BF16)
-        dt[cols:, at] = attended.astype(F32).T.astype(BF16)
+        dt[:, at] = d_qkv.astype(F32).T.astype(BF16)
+        return attended.astype(F32).T.astype(BF16)
+
+    def answer():
+        send_wo.wait_recv()
+        att_to[...] = att_grad(wo_prev)
+        send_att.start()
+
+    def received_att():
+        send_att.wait_recv()
+        return att_from[...]
 
     for load in loads:
         load.wait()
-    differentiate(0, own, lambda c: None, lambda c: None, b)
-
-    differentiate(1, far, lambda c: send_out(0, c).wait_recv(), lambda c: send_out(1, c).wait_recv(), nxt)
-
-    def gradient(i, carry):
-        k = jnp.where(d == n - 1, i, n - 1 - i)
-        gt[k, :cols, :] = dot(dt[:cols, :], xx[:, lanes(k)]).astype(BF16)
-        gt[k, cols:, :] = dot(dt[cols:, :], gg[:, lanes(k)]).astype(BF16)
-
+    pl.when(odd)(answer)
+    turned_att[...] = differentiate(0, own, project(own, lambda c: None), lambda: att_grad(wo), b)
+
+    pl.when(even)(start_x)
+
+    def shard_at(i):
+        return jnp.where(d == n - 1, i, n - 1 - i)
+
+    def out_gradient_back():
+        send_back.wait_recv()
+
+        def step(i, carry):
+            k = shard_at(i)
+            go_to[:, lanes(k)] = dot(back_from[...], gg[:, lanes(k)]).astype(BF16)
+            send_go(k).start()
+            return carry
+
+        lax.fori_loop(0, n, step, 0)
+
+    pl.when(odd)(out_gradient_back)
+
+    back_to[...] = differentiate(1, far, project(far, lambda c: send_x(c).wait_recv()), received_att, nxt)
+    send_back.start()
+
+    def start_sums(k, first, last):
         @pl.when((d == 0) & (k > 0))
         def _():
-            for p in range(PARTS):
+            for p in range(first, last):
                 send_up(k, p).start()
 
         @pl.when((d == n - 1) & (k < n - 1))
         def _():
-            for p in range(PARTS):
+            for p in range(first, last):
                 send_down(k, p).start()
 
-        return carry
-
-    lax.fori_loop(0, n, gradient, 0)
+    def gradient_qkv(i, carry):
+        k = shard_at(i)
+        gt[k, :cols, :] = dot(dt[...], xx[:, lanes(k)]).astype(BF16)
+        start_sums(k, 0, PARTS - 1)
+        return carry
+
+    lax.fori_loop(0, n, gradient_qkv, 0)
+    pl.when(even)(answer)
 
     def far_term(c, carry):
         tsend[:, lanes(c)] = dot_nt(dq[1], w[lanes(c), :]).astype(BF16)
@@ -170,32 +225,53 @@
 
     lax.fori_loop(0, n, far_term, 0)
 
-    def tick(t, carry):
+    def pass_on(t, first, each):
         up, down = t - d, t - (n - 1 - d)
 
-        @pl.when((d > 0) & (up >= 0) & (up < (n - 1 - d) * PARTS))
+        @pl.when((d > 0) & (up >= 0) & (up < (n - 1 - d) * each))
         def _():
-            k, p = n - 1 - up // PARTS, up % PARTS
+            k, p = n - 1 - up // each, first + up % each
             send_up(k, p).wait_recv()
             gt[k, rows(p), :] = (gt[k, rows(p), :].astype(F32) + from_low[k, rows(p), :].astype(F32)).astype(BF16)
             send_up(k, p).start()
 
-        @pl.when((d < n - 1) & (down >= 0) & (down < d * PARTS))
+        @pl.when((d < n - 1) & (down >= 0) & (down < d * each))
         def _():
-            k, p = down // PARTS, down % PARTS
+            k, p = down // each, first + down % each
             send_down(k, p).wait_recv()
             gt[k, rows(p), :] = (gt[k, rows(p), :].astype(F32) + from_high[k, rows(p), :].astype(F32)).astype(BF16)
             send_down(k, p).start()
 
-        return carry
-
-    lax.fori_loop(1, 1 + (n - 2) * PARTS, tick, 0)
+    ticks = 1 + (n - 2) * (PARTS - 1)
+
+    def tick_qkv(t, carry):
+        pass_on(t, 0, PARTS - 1)
+        return carry
+
+    lax.fori_loop(1, ticks, tick_qkv, 0)
 
     def own_term(c, carry):
         term[:, lanes(c)] = dot_nt(dq[0], w[lanes(c), :])
         return carry
 
     lax.fori_loop(0, n, own_term, 0)
+
+    pl.when(even)(out_gradient_back)
+
+    def gradient_out(i, carry):
+        k = shard_at(i)
+        send_go(k).wait_recv()
+        gt[k, cols:, :] = (dot(turned_att[...], gg[:, lanes(k)]) + go_from[:, lanes(k)].astype(F32)).astype(BF16)
+        start_sums(k, PARTS - 1, PARTS)
+        return carry
+
+    lax.fori_loop(0, n, gradient_out, 0)
+
+    def tick_out(t, carry):
+        pass_on(t, PARTS - 1, 1)
+        return carry
+
+    lax.fori_loop(1, n - 1, tick_out, 0)
 
     def store(c):
         return pltpu.make_async_copy(tback.at[:, lanes(c)], ig_hbm.at[:, lanes(c)], store_sem.at[c])
@@ -219,9 +295,12 @@
         else:
             plain[...] = total.astype(BF16)
 
+    send_wo.wait_send()
+    send_att.wait_send()
+    send_back.wait_send()
     for c in range(n):
-        send_out(0, c).wait_send()
-        send_out(1, c).wait_send()
+        send_x(c).wait_send()
+        send_go(c).wait_send()
         send_term(c).wait_send()
         store(c).wait()
         for p in range(PARTS):
@@ -276,6 +355,7 @@
     dma = pltpu.SemaphoreType.DMA
     seq = pltpu.VMEM((count, full), BF16)
     pairs = pltpu.VMEM((2 * count, full), BF16)
+    heads = pltpu.VMEM((head, full), BF16)
     shards = pltpu.VMEM((n, rows, wide), BF16)
     results = (
         jax.ShapeDtypeStruct((count, full), BF16),
@@ -288,15 +368,20 @@
         in_specs=[hbm, hbm, vmem, hbm, hbm],
         out_specs=(hbm, vmem, vmem),
         scratch_shapes=[
-            pairs, pairs,
+            pairs, seq,
             pltpu.VMEM((full, 3 * head), BF16),
-            pltpu.VMEM((head, full), BF16),
-            pltpu.VMEM((rows, 2 * count), BF16),
+            heads, heads, heads, heads,
+            pltpu.VMEM((count, head), BF16),
+            pltpu.VMEM((count, head), BF16),
+            pltpu.VMEM((head, count), BF16),
+            pltpu.VMEM((head, count), BF16),
+            pltpu.VMEM((head, count), BF16),
+            pltpu.VMEM((3 * head, 2 * count), BF16),
             pltpu.VMEM((2, count, 3 * head), BF16),
             shards, shards, shards,
             pltpu.VMEM((count, full), F32),
             seq, seq,
-            dma((4,)), dma((2, n)), dma((2, n)), dma((n,)), dma((n,)),
+            dma((4,)), dma((n,)), dma((n,)), dma((n,)), dma((n,)), dma((2,)), dma((2,)), dma((2,)), dma((n,)), dma((n,)),
             dma((n, PARTS)), dma((n, PARTS)), dma((n, PARTS)), dma((n, PARTS)), dma((n,)),
         ],
         compiler_params=pltpu.CompilerParams(

time: 113 us -> 116 us (1.027)
  Pallas kernels: 112 us -> 115 us
    pallas_call x1, Pallas kernels: 109 us -> 112 us  [local(): pl.pallas_call(functools.partial(kernel, nb, n, wide), out_shape=results,...]
where the time goes in v4:
time: 116 us
  Pallas kernels  115 us (99%)
    pallas_call x1, Pallas kernels, local(): pl.pallas_call(functools.partial(kernel, nb, n, wide), out_shape=results,...  112 us
    pallas_call x1, Pallas kernels, local(): pl.pallas_call(functools.partial(place_kernel, n, wide), out_shape=result...  3.16 us

profile of v4, /device:TPU:1, one launch (start us, length us, event | category | flops | bytes accessed | tf_op | source)
XLA Modules:
  0.0 115.9 jit_solution(3903169105899638932)
XLA Ops:
  0.6 112.1 %shard_map.76 = (bf16[256,5120]{1,0:T(8,128)(2,1)}, bf16[1280,384]{1,0:T(8,128)(2,1)}, bf16[128,1280]{1,0:T(8,128)(2,1)}) custom-call(bf16[256,5120]{1,0:T(8,128)(2,1)} %bitcast.9, bf16[256,5120]{1,0:T(8,128)(2,1)} %bitcast.10, s32[8,256]{1,0:T(8,128)} %bitcast.12, bf16[5120,384]{1,0:T(8,128)(2,1)} %bitcast.8, bf16[128,5120]{1,0:T(8,128)(2,1)} %bitcast.11), custom_call_target="tpu_custom_call" | custom-call | tf_op jit(solution)/shard_map/pallas_call | solution.py:365
  112.8 3.2 %shard_map.77 = (bf16[256,5120]{1,0:T(8,128)(2,1)}, bf16[1280,384]{1,0:T(8,128)(2,1)}, bf16[128,1280]{1,0:T(8,128)(2,1)}) custom-call(bf16[256,5120]{1,0:T(8,128)(2,1)} %get-tuple-element.9.ig_hbm, bf16[1280,384]{1,0:T(8,128)(2,1)} %get-tuple-element.10.qkv_hbm, bf16[128,1280]{1,0:T(8,128)(2,1)} %get-tuple-element.11.out_hbm), custom_call_target="tpu_custom_call" | custom-call | tf_op jit(solution)/shard_map/pallas_call | solution.py:397

commit v5 on v4

--- a/solution.py
+++ b/solution.py
@@ -223,7 +223,10 @@
         send_term(c).start()
         return carry
 
-    lax.fori_loop(0, n, far_term, 0)
+    lax.fori_loop(0, n // 2, far_term, 0)
+
+    def other_half():
+        lax.fori_loop(n // 2, n, far_term, 0)
 
     def pass_on(t, first, each):
         up, down = t - d, t - (n - 1 - d)
@@ -244,7 +247,10 @@
 
     ticks = 1 + (n - 2) * (PARTS - 1)
 
+    between = (d > 0) & (d < n - 1)
+
     def tick_qkv(t, carry):
+        pl.when(between & (t == (1 + ticks) // 2))(other_half)
         pass_on(t, 0, PARTS - 1)
         return carry
 
@@ -266,6 +272,7 @@
         return carry
 
     lax.fori_loop(0, n, gradient_out, 0)
+    pl.when(jnp.logical_not(between))(other_half)
 
     def tick_out(t, carry):
         pass_on(t, PARTS - 1, 1)

time: 116 us -> 116 us (level)
  no operation moved by 1% of the time
where the time goes in v5:
time: 116 us
  Pallas kernels  115 us (99%)
    pallas_call x1, Pallas kernels, local(): pl.pallas_call(functools.partial(kernel, nb, n, wide), out_shape=results,...  112 us
    pallas_call x1, Pallas kernels, local(): pl.pallas_call(functools.partial(place_kernel, n, wide), out_shape=result...  3.16 us

profile of v5, /device:TPU:1, one launch (start us, length us, event | category | flops | bytes accessed | tf_op | source)
XLA Modules:
  0.0 115.8 jit_solution(9712695696134841911)
XLA Ops:
  0.6 112.0 %shard_map.76 = (bf16[256,5120]{1,0:T(8,128)(2,1)}, bf16[1280,384]{1,0:T(8,128)(2,1)}, bf16[128,1280]{1,0:T(8,128)(2,1)}) custom-call(bf16[256,5120]{1,0:T(8,128)(2,1)} %bitcast.9, bf16[256,5120]{1,0:T(8,128)(2,1)} %bitcast.10, s32[8,256]{1,0:T(8,128)} %bitcast.12, bf16[5120,384]{1,0:T(8,128)(2,1)} %bitcast.8, bf16[128,5120]{1,0:T(8,128)(2,1)} %bitcast.11), custom_call_target="tpu_custom_call" | custom-call | tf_op jit(solution)/shard_map/pallas_call | solution.py:372
  112.6 3.2 %shard_map.77 = (bf16[256,5120]{1,0:T(8,128)(2,1)}, bf16[1280,384]{1,0:T(8,128)(2,1)}, bf16[128,1280]{1,0:T(8,128)(2,1)}) custom-call(bf16[256,5120]{1,0:T(8,128)(2,1)} %get-tuple-element.9.ig_hbm, bf16[1280,384]{1,0:T(8,128)(2,1)} %get-tuple-element.10.qkv_hbm, bf16[128,1280]{1,0:T(8,128)(2,1)} %get-tuple-element.11.out_hbm), custom_call_target="tpu_custom_call" | custom-call | tf_op jit(solution)/shard_map/pallas_call | solution.py:404
